TPU v7x, 512 devices: a whole 4x4x16 slice. The times are simulated.
512 devices in a mesh: dp: 64 (over y, z), tensor: 8 (over x, core).
Axes of the slice: x: 4, y: 4, z: 16, core: 2. Of those that a mesh axis runs over, the one named last changes fastest.
Arguments:
- layer_inputs: bfloat16 [3, 16384, 4096], P(None, 'dp', 'tensor'), may hold values from -8 to 8
- layer_outgrads: bfloat16 [3, 16384, 2048], P(None, 'dp', 'tensor'), may hold values from -0.125 to 0.125
- doc_starts: int32 [64, 8], P('dp'), may hold values from 0 to 256, as said below
- row_tokens: int32 [64], P('dp'), may hold values from 64 to 256, as said below
- doc_patient: int32 [64, 8], P('dp'), may hold values from 0 to 127
Outputs:
- weight_grad: float32 [4096, 2048], P('dp', 'tensor')
- doc_scale: float32 [64, 8], P('dp')
Inputs may be any that keep to these rules, and one draw needn't show every extreme that they name: doc_starts[r, 0] = 0 and each row's starts never fall; slot d covers positions doc_starts[r, d] to doc_starts[r, d + 1] - 1, the last slot up to row_tokens[r] - 1; a nonempty slot holds 16 to 64 tokens and every row has one of exactly 64; empty slots start at row_tokens[r]. row_tokens[r] is the end of row r's last nonempty document; later positions are padding.
All inputs are finite; a program needn't handle non-finite values.
Results may differ from a plain program's by a relative error of at most 0.0013.
Values may be sent and summed in bfloat16 or wider, within the bound.
A program may use at most 64 MiB of HBM per device.

v0:
```python
import math

import jax
import jax.numpy as jnp
from jax import lax
from jax.sharding import PartitionSpec as P

D = 4096
LAYERS = 3
DOC_MOST = 64
PAT_DEV = 2
GW = 2048


def row_layout(starts, row_count, row_len):
    positions = jnp.arange(row_len, dtype=jnp.int32)
    doc_of = jnp.sum((starts[None, :] <= positions[:, None]).astype(jnp.int32), axis=1) - 1
    is_valid = positions < row_count
    slots = jnp.arange(starts.shape[0], dtype=jnp.int32)
    member = ((doc_of[:, None] == slots[None, :]) & is_valid[:, None]).astype(jnp.float32)
    same_doc = (
        (doc_of[:, None] == doc_of[None, :]) & is_valid[:, None] & is_valid[None, :]
    ).astype(jnp.float32)
    return (member, same_doc)


def gram_rows(block):
    return lax.dot_general(
        block, block, (((2,), (2,)), ((0,), (0,))), preferred_element_type=jnp.float32
    )


def doc_sums(product, member):
    return jnp.einsum(
        "rt,rtd->rd", jnp.sum(product, axis=2), member, precision=lax.Precision.HIGHEST
    )


def on_device(layer_inputs, layer_outgrads, doc_starts, row_tokens, doc_patient):
    clip_bound = DOC_MOST * math.sqrt(LAYERS * D * GW) / 300.0
    row_local = doc_starts.shape[0]
    tok_local = layer_inputs.shape[1]
    row_len = tok_local // row_local
    member, same_doc = jax.vmap(row_layout, in_axes=(0, 0, None))(doc_starts, row_tokens, row_len)
    next_starts = jnp.concatenate([doc_starts[:, 1:], row_tokens[:, None]], axis=1)
    nonempty = (next_starts > doc_starts).astype(jnp.float32)
    patients = jnp.arange(PAT_DEV * lax.axis_size("dp"), dtype=jnp.int32)
    patient_hits = (doc_patient[:, :, None] == patients[None, None, :]).astype(jnp.float32)
    local_counts = jnp.sum(patient_hits * nonempty[:, :, None], axis=(0, 1))
    counts = lax.psum(local_counts, "dp")
    first_inputs = lax.all_gather(layer_inputs[0], "tensor", axis=1, tiled=True)

    def split_rows(block):
        return block.reshape(row_local, row_len, block.shape[-1])

    doc_norms = jnp.zeros((row_local, doc_starts.shape[1]), jnp.float32)
    for which_layer in range(LAYERS):
        input_gram, grad_gram = lax.psum(
            (
                gram_rows(split_rows(layer_inputs[which_layer])),
                gram_rows(split_rows(layer_outgrads[which_layer])),
            ),
            "tensor",
        )
        doc_norms = doc_norms + doc_sums(same_doc * input_gram * grad_gram, member)
    doc_count = jnp.sum(patient_hits * counts[None, None, :], axis=2)
    doc_scale = (
        clip_bound / jnp.maximum(clip_bound, jnp.sqrt(doc_norms)) / jnp.maximum(doc_count, 1.0)
    )
    token_weight = jnp.einsum(
        "rtd,rd->rt", member, doc_scale, precision=lax.Precision.HIGHEST
    ).reshape(tok_local)
    weighted = (token_weight[:, None] * layer_outgrads[0]).astype(jnp.bfloat16)
    weight_grad = lax.psum_scatter(
        lax.dot_general(
            first_inputs, weighted, (((0,), (0,)), ((), ())), preferred_element_type=jnp.float32
        ),
        "dp",
        scatter_dimension=0,
        tiled=True,
    )
    return (weight_grad, doc_scale)


def solution(mesh):
    placed = (
        P(None, "dp", "tensor"),
        P(None, "dp", "tensor"),
        P("dp", None),
        P("dp"),
        P("dp", None),
    )
    return jax.shard_map(
        on_device,
        mesh=mesh,
        in_specs=placed,
        out_specs=(P("dp", "tensor"), P("dp", None)),
        check_vma=False,
    )
```

profile of v0, /device:TPU:2, one launch (start us, length us, event | category | flops | bytes accessed | tf_op | source)
XLA Modules:
  0.0 879.2 jit_solution(13097255916912389009)
XLA Ops:
  7.2 0.0 copy-start
  7.2 0.0 all-reduce.3.cloned.1.call-start
  7.2 2.1 convolution_bitcast_fusion.3
  9.3 2.0 convolution_bitcast_fusion.1
  11.3 0.0 copy-start.1
  11.3 0.0 copy-start.2
  11.3 2.0 convolution_bitcast_fusion.2
  13.3 1.9 convolution_bitcast_fusion.6
  15.2 1.9 convolution_bitcast_fusion.4
  17.1 0.0 copy-done
  17.1 0.9 convolution_bitcast_fusion.5
  18.1 0.0 all-reduce.3.cloned.1.call-update
  18.1 0.0 all-gather.3.cloned.1.call-start
  18.1 1.7 slice.23
  19.8 0.0 all-gather.3.cloned.1.call-update
  19.8 0.0 reduce-scatter.4.cloned.1.call-start
  20.5 0.0 copy-done.1
  20.5 0.1 slice.29
  20.6 0.1 fusion.35
  20.7 0.0 copy-done.2
  20.7 0.1 select_reduce_fusion.1
  20.8 149.9 %psum.55 = f32[128]{0:T(128)S(1)} all-reduce(f32[128]{0:T(128)S(1)} %select_reduce_fusion.1), channel_id=1, replica_groups=mesh['dp'=64,'tensor'=8] {'dp'}, use_global_device_ids=true, to_apply=%region_11.0 | all-reduce | flops 128 | bytes 1024 | tf_op jit(solution)/shard_map/psum | solution.py:50
  170.7 0.1 convert_reduce_fusion
  170.7 0.2 select_reduce_fusion
  170.9 0.0 all-reduce.3.cloned.1.call-done
  171.0 1.6 multiply_reduce_fusion.2
  172.6 0.3 convolution_bitcast_fusion.8
  172.9 0.3 convolution_bitcast_fusion.7
  173.1 0.3 fusion.6
  173.4 0.0 copy-start.3
  173.4 0.2 fusion.20
  173.7 0.0 all-gather.3.cloned.1.call-done
  173.7 4.4 convolution_bitcast_fusion
  178.1 0.0 copy-done.3
  178.1 5.6 copy.10
  183.7 0.0 reduce-scatter.4.cloned.1.call-update
  183.7 688.9 %reduce-scatter.4.cloned.1.call-done = f32[64,256]{1,0:T(8,128)} async-done(((f32[4096,256]{1,0:T(8,128)}), f32[64,256]{1,0:T(8,128)}) %reduce-scatter.4.cloned.1.call-update) | async-done | bytes 65552
  (2 shorter events, 0.0 us)
Async XLA Ops:
  7.2 10.0 %copy-start = (bf16[3,256,256]{2,1,0:T(8,128)(2,1)S(1)}, bf16[3,256,256]{2,1,0:T(8,128)(2,1)}, u32[]{:S(2)}) copy-start(bf16[3,256,256]{2,1,0:T(8,128)(2,1)} %param.6) | copy-start | bytes 1179652
  7.2 163.8 %all-reduce.3.cloned.1.call-start = ((), (), s32[]{:S(2)}) async-start(), calls=%async_computation.3 | async-start | bytes 3145728 | tf_op jit(solution)/shard_map/psum | solution.py:58
  11.3 9.2 %copy-start.1 = (s32[1,8]{1,0:T(1,128)S(1)}, s32[1,8]{1,0:T(1,128)}, u32[]{:S(2)}) copy-start(s32[1,8]{1,0:T(1,128)} %param.7) | copy-start | bytes 100
  11.3 9.4 %copy-start.2 = (s32[1,8]{1,0:T(1,128)S(1)}, s32[1,8]{1,0:T(1,128)}, u32[]{:S(2)}) copy-start(s32[1,8]{1,0:T(1,128)} %param.9) | copy-start | bytes 100
  18.1 155.6 %all-gather.3.cloned.1.call-start = ((), (), s32[]{:S(2)}) async-start(), calls=%async_computation.1 | async-start | bytes 2359296 | tf_op jit(solution)/shard_map/all_gather | solution.py:51
  19.8 852.8 %reduce-scatter.4.cloned.1.call-start = ((), (), s32[]{:S(2)}) async-start(), calls=%async_computation.2 | async-start | bytes 4259840
  173.4 4.7 copy-start.3
Sparse Core Ops, SparseCore 0:
  18.2 81.9 all-reduce.2
  102.4 34.0 all-gather.2
  183.8 688.7 reduce-scatter.3
where the time goes:
time: 880 us; the launch traced here: 879 us
  waiting for transfers between devices  689 us (78%)
  blocking collectives  150 us (17%)
  matrix products  16.3 us (2%)
  between operations  14.4 us (2%)
    unnamed x4, waiting for transfers between devices  689 us
    psum x1, blocking collectives, on_device(): counts = lax.psum(local_counts, 'dp')  150 us
  transfers between devices with their start and end apart: 3, of which 1 were waited for; matrix products, arithmetic and copies ran while one was open for 1% of the time, Pallas kernels for 0%

commit v1 on v0

v1 whole, which is shorter than its diff:
```python
import functools
import math

import jax
import jax.numpy as jnp
from jax import lax
from jax.experimental import pallas as pl
from jax.experimental.pallas import tpu as pltpu
from jax.sharding import PartitionSpec as P

D = 4096
LAYERS = 3
DOC_MOST = 64
GW = 2048
MAXDOC = 8
TOK = 256
NX = 4
NY = 4
NT = 2 * NX
PIECES = 2
MESH = pl.DeviceIdType.MESH
F32 = jnp.float32
BF16 = jnp.bfloat16


def remote(src, dst, send_sem, recv_sem, device):
    return pltpu.make_async_remote_copy(
        src_ref=src,
        dst_ref=dst,
        send_sem=send_sem,
        recv_sem=recv_sem,
        device_id=device,
        device_id_type=MESH,
    )


def pack_band(gram):
    shape = (64, 128)
    row = lax.broadcasted_iota(jnp.int32, shape, 0)
    lane = lax.broadcasted_iota(jnp.int32, shape, 1)
    upper = lax.rem(lane, 64) >= row
    low_lanes = lane < 64
    halves = []
    for q in range(2):
        base = 128 * q
        first = gram[base : base + 64, base : base + 128]
        second = gram[base + 64 : base + 128, base : base + 128]
        block0 = jnp.where(upper, first, pltpu.roll(first, 64, 1))
        if q == 0:
            across = pltpu.roll(gram[base + 64 : base + 128, base + 128 : base + 256], 64, 1)
        else:
            across = jnp.zeros(shape, F32)
        block1 = jnp.where(upper, second, across)
        halves.append(jnp.where(low_lanes, block0, block1))
    return halves


def gram_of(block):
    return lax.dot_general(block, block, (((1,), (1,)), ((), ())), preferred_element_type=F32)


def kernel(
    nz,
    clip_bound,
    xi_ref,
    g_ref,
    starts_ref,
    rows_ref,
    pat_ref,
    out_ref,
    scale_ref,
    xt,
    xs,
    gy,
    wy,
    gp,
    gr,
    npr,
    hy,
    hz,
    t3,
    part,
    rd,
    ru,
    sc_send,
    sc_recv,
    g_send,
    g_recv,
    hy_send,
    hy_recv,
    hz_send,
    hz_recv,
    gr_send,
    gr_recv,
    np_send,
    np_recv,
    t3_send,
    t3_recv,
    ag_send,
    ag_recv,
    sib_send,
    sib_recv,
    dn_send,
    dn_recv,
    up_send,
    up_recv,
):
    dp = lax.axis_index("dp")
    tensor = lax.axis_index("tensor")
    y = lax.div(dp, nz)
    z = lax.rem(dp, nz)
    x = lax.div(tensor, 2)
    c = lax.rem(tensor, 2)

    def device(yy, zz, xx, cc):
        return (yy * nz + zz, xx * 2 + cc)

    def y_peer(off):
        return device(lax.rem(y + off, NY), z, x, c)

    def z_peer(off):
        return device(y, lax.rem(z + off, nz), x, c)

    def t_peer(off):
        return (dp, lax.rem(tensor + off, NT))

    def x_peer(off):
        return device(y, z, lax.rem(x + off, NX), c)

    sibling = device(y, z, x, 1 - c)
    on_diagonal = x == y

    barrier = pltpu.get_barrier_semaphore()

    def greet(target):
        pl.semaphore_signal(barrier, inc=1, device_id=target, device_id_type=MESH)

    for off in range(1, NT):
        greet(t_peer(off))
    for off in range(1, NY):
        greet(y_peer(off))
    for off in range(1, nz):
        greet(z_peer(off))
    for off in range(1, NX):
        greet(device(x, z, lax.rem(x + off, NX), c))
        greet(device(lax.rem(y + off, NY), z, y, c))

    @pl.when(jnp.logical_not(on_diagonal))
    def _():
        greet(device(x, z, x, c))
        greet(device(y, z, y, c))

    xt[...] = xi_ref[0].T

    starts = [starts_ref[0, d] for d in range(MAXDOC)]
    used = rows_ref[0]
    ends = [jnp.minimum(starts[d + 1], used) if d + 1 < MAXDOC else used for d in range(MAXDOC)]
    patients = [pat_ref[0, d] for d in range(MAXDOC)]
    tile = (8, 128)
    sub8 = lax.broadcasted_iota(jnp.int32, tile, 0)
    lane8 = lax.broadcasted_iota(jnp.int32, tile, 1)
    hist = jnp.zeros(tile, F32)
    patient_of = jnp.zeros(tile, jnp.int32)
    for d in range(MAXDOC):
        nonempty = jnp.where(ends[d] > starts[d], 1.0, 0.0)
        hist = hist + jnp.where(lane8 == patients[d], nonempty, 0.0)
        patient_of = jnp.where(sub8 == d, patients[d], patient_of)
    hy[y] = hist
    gy[y] = g_ref[0]

    pl.semaphore_wait(barrier, NT + NY + nz - 3 + jnp.where(on_diagonal, 2 * (NX - 1), 2 * NX))

    scatter = [
        remote(
            xt.at[pl.ds(pl.multiple_of(lax.rem(x + off, NX) * 128, 128), 128)],
            xs.at[lax.rem(x + off, NX) * 2 + c, y],
            sc_send.at[off],
            sc_recv.at[y],
            device(x, z, lax.rem(x + off, NX), c),
        )
        for off in range(NX)
    ]
    own_piece = pltpu.make_async_copy(
        xt.at[pl.ds(pl.multiple_of(x * 128, 128), 128)], xs.at[tensor, y], sc_recv.at[y]
    )
    for off in range(1, NX):
        scatter[off].start()

    @pl.when(jnp.logical_not(on_diagonal))
    def _():
        scatter[0].start()

    @pl.when(on_diagonal)
    def _():
        own_piece.start()

    hist_y = [
        remote(hy.at[y], hy.at[y], hy_send.at[off], hy_recv.at[off], y_peer(off))
        for off in range(1, NY)
    ]
    for copy in hist_y:
        copy.start()
    outgrads = [
        remote(g_ref.at[0], gy.at[y], g_send.at[off], g_recv.at[off], y_peer(off))
        for off in range(1, NY)
    ]
    for copy in outgrads:
        copy.start()

    for layer in range(LAYERS):
        for which, ref in ((0, xi_ref), (1, g_ref)):
            low, high = pack_band(gram_of(ref[layer]))
            for owner in range(NT):
                source = low if owner < 4 else high
                first = (owner % 4) * 16
                gp[owner, 2 * layer + which] = source[first : first + 16]
    grams = [
        remote(
            gp.at[lax.rem(tensor + off, NT)],
            gr.at[tensor],
            gr_send.at[off],
            gr_recv.at[off],
            t_peer(off),
        )
        for off in range(1, NT)
    ]
    for copy in grams:
        copy.start()

    gathers = []
    for yy in range(NY):
        remote(
            xs.at[tensor, yy], xs.at[tensor, yy], sc_send.at[0], sc_recv.at[yy], sibling
        ).wait_recv()
        block = xs.at[tensor, yy]
        copies = [
            remote(block, block, ag_send.at[0, yy], ag_recv.at[0, yy], x_peer(1)),
            remote(block, block, ag_send.at[1, yy], ag_recv.at[1, yy], x_peer(NX - 1)),
            remote(block, block, sib_send.at[0, yy], sib_recv.at[0, yy], sibling),
        ]
        for copy in copies:
            copy.start()
        gathers += copies

    for off in range(1, NY):
        slot = hy.at[lax.rem(y + NY - off, NY)]
        remote(slot, slot, hy_send.at[off], hy_recv.at[off], y_peer(off)).wait_recv()
    hz[z] = hy[0] + hy[1] + hy[2] + hy[3]
    hist_z = [
        remote(hz.at[z], hz.at[z], hz_send.at[off], hz_recv.at[off], z_peer(off))
        for off in range(1, nz)
    ]
    for copy in hist_z:
        copy.start()

    total = gp[tensor]
    for off in range(1, NT):
        source = lax.rem(tensor + NT - off, NT)
        remote(
            gr.at[source], gr.at[source], gr_send.at[off], gr_recv.at[off], t_peer(off)
        ).wait_recv()
        total = total + gr[source]
    product = total[0] * total[1] + total[2] * total[3] + total[4] * total[5]
    band = (16, 128)
    packed_row = lax.broadcasted_iota(jnp.int32, band, 0) + tensor * 16
    packed_lane = lax.broadcasted_iota(jnp.int32, band, 1)
    inner_row = lax.rem(packed_row, 64)
    inner_lane = lax.rem(packed_lane, 64)
    base = 64 * (2 * lax.div(packed_row, 64) + lax.div(packed_lane, 64))
    tok_t = base + inner_row
    tok_s = base + inner_lane + jnp.where(inner_lane >= inner_row, 0, 64)
    product = product * jnp.where(tok_t == tok_s, 1.0, 2.0)
    norm_part = jnp.zeros(tile, F32)
    for d in range(MAXDOC):
        inside = (
            (tok_t >= starts[d]) & (tok_t < ends[d]) & (tok_s >= starts[d]) & (tok_s < ends[d])
        )
        value = jnp.sum(jnp.where(inside, product, 0.0), keepdims=True)
        norm_part = jnp.where(sub8 == d, value, norm_part)
    npr[tensor] = norm_part
    norms_out = [
        remote(npr.at[tensor], npr.at[tensor], np_send.at[off], np_recv.at[off], t_peer(off))
        for off in range(1, NT)
    ]
    for copy in norms_out:
        copy.start()

    def arrived(hop, yy, source_x, recv_slot):
        slot = xs.at[source_x * 2 + c, yy]
        remote(slot, slot, ag_send.at[hop, yy], recv_slot, sibling).wait_recv()
        return slot

    left_x = lax.rem(x + NX - 1, NX)
    right_x = lax.rem(x + 1, NX)
    far_x = lax.rem(x + 2, NX)
    for yy in range(NY):
        block = arrived(0, yy, left_x, ag_recv.at[0, yy])
        if yy < NY // 2:
            copy = remote(block, block, ag_send.at[2, yy], ag_recv.at[2, yy], x_peer(1))
            copy.start()
            gathers.append(copy)
        copy = remote(block, block, sib_send.at[1, yy], sib_recv.at[1, yy], sibling)
        copy.start()
        gathers.append(copy)
        block = arrived(1, yy, right_x, ag_recv.at[1, yy])
        if yy >= NY // 2:
            copy = remote(block, block, ag_send.at[2, yy], ag_recv.at[2, yy], x_peer(NX - 1))
            copy.start()
            gathers.append(copy)
        copy = remote(block, block, sib_send.at[2, yy], sib_recv.at[2, yy], sibling)
        copy.start()
        gathers.append(copy)

    for off in range(1, nz):
        slot = hz.at[lax.rem(z + nz - off, nz)]
        remote(slot, slot, hz_send.at[off], hz_recv.at[off], z_peer(off)).wait_recv()
    counts = hz[0]
    for zz in range(1, nz):
        counts = counts + hz[zz]
    doc_count = jnp.sum(jnp.where(lane8 == patient_of, counts, 0.0), axis=1, keepdims=True)
    for off in range(1, NT):
        slot = npr.at[lax.rem(tensor + NT - off, NT)]
        remote(slot, slot, np_send.at[off], np_recv.at[off], t_peer(off)).wait_recv()
    norms = npr[0]
    for tt in range(1, NT):
        norms = norms + npr[tt]
    scale = clip_bound / jnp.maximum(clip_bound, jnp.sqrt(norms)) / jnp.maximum(doc_count, 1.0)
    scale_row = jnp.sum(jnp.where(sub8 == lane8, scale, 0.0), axis=0, keepdims=True)
    scale_ref[...] = scale_row[:, :MAXDOC]
    told = jnp.where(sub8 == 2, scale_row, 0.0)
    for d in range(MAXDOC):
        told = jnp.where((sub8 == 0) & (lane8 == d), starts[d].astype(F32), told)
        told = jnp.where((sub8 == 1) & (lane8 == d), ends[d].astype(F32), told)
    t3[y] = told
    told_out = [
        remote(t3.at[y], t3.at[y], t3_send.at[off], t3_recv.at[off], y_peer(off))
        for off in range(1, NY)
    ]
    for copy in told_out:
        copy.start()

    for yy in range(NY):
        block = arrived(2, yy, far_x, ag_recv.at[2, yy])
        copy = remote(block, block, sib_send.at[3, yy], sib_recv.at[3, yy], sibling)
        copy.start()
        gathers.append(copy)

    for off in range(1, NY):
        source = lax.rem(y + NY - off, NY)
        slot = gy.at[source]
        remote(slot, slot, g_send.at[off], g_recv.at[off], y_peer(off)).wait_recv()
        slot = t3.at[source]
        remote(slot, slot, t3_send.at[off], t3_recv.at[off], y_peer(off)).wait_recv()
    token = lax.broadcasted_iota(jnp.int32, (TOK, 128), 0).astype(F32)
    for yy in range(NY):
        inside = (token >= t3[yy, 0:1, :]) & (token < t3[yy, 1:2, :])
        weight = jnp.sum(jnp.where(inside, t3[yy, 2:3, :], 0.0), axis=1, keepdims=True)
        wy[yy] = (weight * gy[yy].astype(F32)).astype(BF16)

    for hop, source_x in enumerate((x, left_x, right_x, far_x)):
        for yy in range(NY):
            slot = xs.at[source_x * 2 + 1 - c, yy]
            remote(slot, slot, sib_send.at[hop, yy], sib_recv.at[hop, yy], sibling).wait_recv()

    for tt in range(NT):
        sums = jnp.dot(xs[tt, 0], wy[0], preferred_element_type=F32)
        for yy in range(1, NY):
            sums = sums + jnp.dot(xs[tt, yy], wy[yy], preferred_element_type=F32)
        owner = 8 * (tt % 2) + 2 * (tt // 2)
        part[owner] = sums[:64]
        part[owner + 1] = sums[64:]

    below, above = z_peer(nz - 1), z_peer(1)
    half = nz // 2
    rows = 64 // PIECES
    chain = []

    def step(s, owner, arrivals, send, recv, target):
        for j in range(PIECES):
            span = pl.ds(j * rows, rows)
            mine = part.at[owner, span]
            if s > 0:
                slot = arrivals.at[s - 1, span]
                remote(slot, slot, send.at[s - 1, j], recv.at[s - 1, j], target).wait_recv()
                mine[...] += slot[...]
            copy = remote(mine, arrivals.at[s, span], send.at[s, j], recv.at[s, j], target)
            copy.start()
            chain.append(copy)

    for s in range(half):
        step(s, lax.rem(z + nz - half + s, nz), rd, dn_send, dn_recv, below)
        if s < half - 1:
            step(s, lax.rem(z + half - 1 - s, nz), ru, up_send, up_recv, above)
    for j in range(PIECES):
        span = pl.ds(j * rows, rows)
        last_up = ru.at[half - 2, span]
        remote(
            last_up, last_up, up_send.at[half - 2, j], up_recv.at[half - 2, j], above
        ).wait_recv()
        last_down = rd.at[half - 1, span]
        remote(
            last_down, last_down, dn_send.at[half - 1, j], dn_recv.at[half - 1, j], below
        ).wait_recv()
        out_ref[span, :] = part[z, span, :] + last_up[...] + last_down[...]

    for off in range(1, NX):
        scatter[off].wait_send()

    @pl.when(jnp.logical_not(on_diagonal))
    def _():
        scatter[0].wait_send()

    for copy in hist_y + outgrads + grams + gathers + hist_z + norms_out + told_out + chain:
        copy.wait_send()


def on_device(nz, layer_inputs, layer_outgrads, doc_starts, row_tokens, doc_patient):
    clip_bound = DOC_MOST * math.sqrt(LAYERS * D * GW) / 300.0
    half = nz // 2
    vmem = pl.BlockSpec(memory_space=pltpu.VMEM)
    smem = pl.BlockSpec(memory_space=pltpu.SMEM)
    dma = pltpu.SemaphoreType.DMA
    return pl.pallas_call(
        functools.partial(kernel, nz, clip_bound),
        out_shape=(
            jax.ShapeDtypeStruct((64, 256), F32),
            jax.ShapeDtypeStruct((1, MAXDOC), F32),
        ),
        in_specs=[vmem, vmem, smem, smem, smem],
        out_specs=(vmem, vmem),
        scratch_shapes=[
            pltpu.VMEM((512, TOK), BF16),
            pltpu.VMEM((NT, NY, 128, TOK), BF16),
            pltpu.VMEM((NY, TOK, 256), BF16),
            pltpu.VMEM((NY, TOK, 256), BF16),
            pltpu.VMEM((NT, 6, 16, 128), F32),
            pltpu.VMEM((NT, 6, 16, 128), F32),
            pltpu.VMEM((NT, 8, 128), F32),
            pltpu.VMEM((NY, 8, 128), F32),
            pltpu.VMEM((nz, 8, 128), F32),
            pltpu.VMEM((NY, 8, 128), F32),
            pltpu.VMEM((nz, 64, 256), F32),
            pltpu.VMEM((half, 64, 256), F32),
            pltpu.VMEM((half - 1, 64, 256), F32),
            dma((NX,)),
            dma((NY,)),
            dma((NY,)),
            dma((NY,)),
            dma((NY,)),
            dma((NY,)),
            dma((nz,)),
            dma((nz,)),
            dma((NT,)),
            dma((NT,)),
            dma((NT,)),
            dma((NT,)),
            dma((NY,)),
            dma((NY,)),
            dma((3, NY)),
            dma((3, NY)),
            dma((4, NY)),
            dma((4, NY)),
            dma((half, PIECES)),
            dma((half, PIECES)),
            dma((half - 1, PIECES)),
            dma((half - 1, PIECES)),
        ],
        compiler_params=pltpu.CompilerParams(
            collective_id=0, has_side_effects=True, vmem_limit_bytes=40 * 1024 * 1024
        ),
    )(layer_inputs, layer_outgrads, doc_starts, row_tokens, doc_patient)


def solution(mesh):
    placed = (
        P(None, "dp", "tensor"),
        P(None, "dp", "tensor"),
        P("dp", None),
        P("dp"),
        P("dp", None),
    )
    return jax.shard_map(
        functools.partial(on_device, mesh.shape["dp"] // NY),
        mesh=mesh,
        in_specs=placed,
        out_specs=(P("dp", "tensor"), P("dp", None)),
        check_vma=False,
    )
```

time: 880 us -> 69.5 us (0.08)
  waiting for transfers between devices: 689 us -> 0 us
  blocking collectives: 150 us -> 0 us
  Pallas kernels: 0 us -> 64.6 us
  matrix products: 16.3 us -> 0 us
  between operations: 14.4 us -> 1.34 us
    unnamed x4 -> x0, waiting for transfers between devices: 689 us -> none
    psum x1 -> x0, blocking collectives: 150 us -> none  [on_device(): counts = lax.psum(local_counts, 'dp')]
    pallas_call x0 -> x1, Pallas kernels: none -> 64.6 us  [on_device(): pl.pallas_call(functools.partial(kernel, nz, clip_bound), out_shape=(jax....]
    dot_general x11 -> x0, matrix products: 16.3 us -> none  [the longest x6 10.8 us: gram_rows(): lax.dot_general(block, block, (((2,), (2,)), ((0,), (0,))), preferred_ele...]
  transfers between devices with their start and end apart: 3 -> 0, of which waited for: 1 -> 0; matrix products, arithmetic and copies ran while one was open for 1% -> 0% of each run, Pallas kernels for 0% -> 0%
where the time goes in v1:
time: 69.5 us; the launch traced here: 69.3 us
  Pallas kernels  64.6 us (93%)
  local copies, waits for them, and re-layouts  3.27 us (5%)
  between operations  1.34 us (2%)
    pallas_call x1, Pallas kernels, on_device(): pl.pallas_call(functools.partial(kernel, nz, clip_bound), out_shape=(jax....  64.6 us
    unnamed x10, local copies, waits for them, and re-layouts  3.27 us

profile of v1, /device:TPU:2, one launch (start us, length us, event | category | flops | bytes accessed | tf_op | source)
XLA Modules:
  0.0 69.3 jit_solution(2554425836684025664)
XLA Ops:
  0.6 0.0 copy-start.3
  0.6 0.0 copy-start.2
  1.3 0.0 copy-done.3
  1.3 0.0 copy-done.2
  1.3 0.0 copy-start
  1.3 1.1 %copy-done = bf16[3,256,512]{2,1,0:T(8,128)(2,1)S(1)} copy-done((bf16[3,256,512]{2,1,0:T(8,128)(2,1)S(1)}, bf16[3,256,512]{2,1,0:T(8,128)(2,1)}, u32[]{:S(2)}) %copy-start) | copy-done | bytes 786456
  2.5 0.0 copy-start.1
  2.5 1.0 %copy-done.1 = bf16[3,256,256]{2,1,0:T(8,128)(2,1)S(1)} copy-done((bf16[3,256,256]{2,1,0:T(8,128)(2,1)S(1)}, bf16[3,256,256]{2,1,0:T(8,128)(2,1)}, u32[]{:S(2)}) %copy-start.1) | copy-done | bytes 393240
  3.5 64.6 %shard_map.68 = (f32[64,256]{1,0:T(8,128)S(1)}, f32[1,8]{1,0:T(1,128)S(1)}) custom-call(bf16[3,256,512]{2,1,0:T(8,128)(2,1)S(1)} %copy-done, bf16[3,256,256]{2,1,0:T(8,128)(2,1)S(1)} %copy-done.1, s32[1,8]{1,0:T(1,128)S(1)} %copy-done.2, s32[1]{0:T(128)S(6)} %copy.9.rows_ref, s32[1,8]{1,0:T(1,128)S(1)} %copy-done.3), custom_call_target="tpu_custom_call" | custom-call | tf_op jit(solution)/shard_map/pallas_call | solution.py:423
  68.1 0.6 copy.10
  68.8 0.5 copy.11
Async XLA Ops:
  0.6 0.7 copy-start.3
  0.6 0.7 copy-start.2
  1.3 1.1 %copy-start = (bf16[3,256,512]{2,1,0:T(8,128)(2,1)S(1)}, bf16[3,256,512]{2,1,0:T(8,128)(2,1)}, u32[]{:S(2)}) copy-start(bf16[3,256,512]{2,1,0:T(8,128)(2,1)} %xi_ref.1) | copy-start | bytes 2359300
  2.5 1.0 %copy-start.1 = (bf16[3,256,256]{2,1,0:T(8,128)(2,1)S(1)}, bf16[3,256,256]{2,1,0:T(8,128)(2,1)}, u32[]{:S(2)}) copy-start(bf16[3,256,256]{2,1,0:T(8,128)(2,1)} %g_ref.1) | copy-start | bytes 1179652

commit v2 on v0

v2 whole, which is shorter than its diff:
```python
import functools
import math

import jax
import jax.numpy as jnp
from jax import lax
from jax.experimental import pallas as pl
from jax.experimental.pallas import tpu as pltpu
from jax.sharding import PartitionSpec as P

D = 4096
LAYERS = 3
DOC_MOST = 64
GW = 2048
MAXDOC = 8
TOK = 256
NX = 4
NY = 4
NT = 2 * NX
WINDOW = (0, 1, -1, 2)
NW = len(WINDOW)
PIECE = 128 // NW
BLOCKS = 4
PIECES = 2
GRAM_TYPE = jnp.float32
MESH = pl.DeviceIdType.MESH
F32 = jnp.float32
BF16 = jnp.bfloat16


def remote(src, dst, send_sem, recv_sem, device):
    return pltpu.make_async_remote_copy(
        src_ref=src,
        dst_ref=dst,
        send_sem=send_sem,
        recv_sem=recv_sem,
        device_id=device,
        device_id_type=MESH,
    )


def pack_band(gram):
    shape = (64, 128)
    row = lax.broadcasted_iota(jnp.int32, shape, 0)
    lane = lax.broadcasted_iota(jnp.int32, shape, 1)
    upper = lax.rem(lane, 64) >= row
    low_lanes = lane < 64
    halves = []
    for q in range(2):
        base = 128 * q
        first = gram[base : base + 64, base : base + 128]
        second = gram[base + 64 : base + 128, base : base + 128]
        block0 = jnp.where(upper, first, pltpu.roll(first, 64, 1))
        if q == 0:
            across = pltpu.roll(gram[base + 64 : base + 128, base + 128 : base + 256], 64, 1)
        else:
            across = jnp.zeros(shape, F32)
        block1 = jnp.where(upper, second, across)
        halves.append(jnp.where(low_lanes, block0, block1))
    return halves


def gram_of(block):
    return lax.dot_general(block, block, (((1,), (1,)), ((), ())), preferred_element_type=F32)


def kernel(
    nz,
    clip_bound,
    xi_ref,
    g_ref,
    starts_in,
    rows_in,
    pat_in,
    out_ref,
    scale_ref,
    starts_ref,
    rows_ref,
    pat_ref,
    xv,
    gv,
    xt,
    xs,
    gy,
    wy,
    gp,
    gr,
    npr,
    hist,
    ring,
    told,
    part,
    rd,
    ru,
    in_sem,
    sc_send,
    sc_recv,
    gz_send,
    gz_recv,
    gy_send,
    gy_recv,
    gf_send,
    gf_recv,
    hist_send,
    hist_recv,
    ring_send,
    ring_recv,
    gr_send,
    gr_recv,
    np_send,
    np_recv,
    told_send,
    told_recv,
    ag_send,
    ag_recv,
    sib_send,
    sib_recv,
    dn_send,
    dn_recv,
    up_send,
    up_recv,
):
    dp = lax.axis_index("dp")
    tensor = lax.axis_index("tensor")
    y = lax.div(dp, nz)
    z = lax.rem(dp, nz)
    x = lax.div(tensor, 2)
    c = lax.rem(tensor, 2)
    members = nz // NW
    place = lax.div(z, NW)

    def device(yy, zz, xx, cc):
        return (yy * nz + zz, xx * 2 + cc)

    def z_at(off):
        return lax.rem(z + off + nz, nz)

    def y_at(off):
        return lax.rem(y + off + NY, NY)

    def x_at(off):
        return lax.rem(x + off + NX, NX)

    def t_at(off):
        return lax.rem(tensor + off + NT, NT)

    def x_peer(off):
        return device(y, z, x_at(off), c)

    def y_peer(off):
        return device(y_at(off), z, x, c)

    sibling = device(y, z, x, 1 - c)
    below, above = device(y, z_at(-NW), x, c), device(y, z_at(NW), x, c)
    on_diagonal = x == y
    window_pairs = [(wi, off) for wi in range(NW) for off in range(NY) if (wi, off) != (0, 0)]
    piece_pairs = [(wi, off) for wi in range(NW) for off in range(NX) if (wi, off) != (0, 0)]

    barrier = pltpu.get_barrier_semaphore()

    def greet(target):
        pl.semaphore_signal(barrier, inc=1, device_id=target, device_id_type=MESH)

    for off in range(1, NT):
        greet((dp, t_at(off)))
    for wi, off in window_pairs:
        greet(device(y_at(off), z_at(-WINDOW[wi]), x, c))
        greet(device(y_at(-off), z_at(WINDOW[wi]), x, c))
    for wi, off in piece_pairs:
        greet(device(x, z_at(-WINDOW[wi]), x_at(off), c))
        greet(device(y_at(off), z_at(WINDOW[wi]), y, c))
    greet(below)
    greet(above)

    @pl.when(jnp.logical_not(on_diagonal))
    def _():
        greet(device(x, z, x, c))
        greet(device(y, z, y, c))

    greetings = NT - 1 + 2 * len(window_pairs) + 2 * len(piece_pairs) + 2

    own_grads = gy.at[0, y]
    loads = [
        pltpu.make_async_copy(xi_ref.at[0], xv.at[0], in_sem.at[0]),
        pltpu.make_async_copy(g_ref.at[0], own_grads, in_sem.at[1]),
        pltpu.make_async_copy(starts_in, starts_ref, in_sem.at[2]),
        pltpu.make_async_copy(rows_in, rows_ref, in_sem.at[3]),
        pltpu.make_async_copy(pat_in, pat_ref, in_sem.at[4]),
        pltpu.make_async_copy(xi_ref.at[pl.ds(1, 2)], xv.at[pl.ds(1, 2)], in_sem.at[5]),
        pltpu.make_async_copy(g_ref.at[pl.ds(1, 2)], gv, in_sem.at[6]),
    ]
    for copy in loads:
        copy.start()

    for copy in loads[2:5]:
        copy.wait()
    starts = [starts_ref[0, d] for d in range(MAXDOC)]
    used = rows_ref[0]
    ends = [jnp.minimum(starts[d + 1], used) if d + 1 < MAXDOC else used for d in range(MAXDOC)]
    patients = [pat_ref[0, d] for d in range(MAXDOC)]
    tile = (8, 128)
    sub8 = lax.broadcasted_iota(jnp.int32, tile, 0)
    lane8 = lax.broadcasted_iota(jnp.int32, tile, 1)
    own_hist = jnp.zeros(tile, F32)
    patient_of = jnp.zeros(tile, jnp.int32)
    for d in range(MAXDOC):
        nonempty = jnp.where(ends[d] > starts[d], 1.0, 0.0)
        own_hist = own_hist + jnp.where(lane8 == patients[d], nonempty, 0.0)
        patient_of = jnp.where(sub8 == d, patients[d], patient_of)
    hist[0, y] = own_hist

    def put_gram(which, block):
        low, high = pack_band(gram_of(block))
        for owner in range(NT):
            source = low if owner < 4 else high
            first = (owner % 4) * 16
            gp[owner, which] = source[first : first + 16].astype(GRAM_TYPE)

    loads[0].wait()
    xt[...] = xv[0].T
    put_gram(0, xv[0])
    loads[1].wait()
    put_gram(1, gy[0, y])
    loads[5].wait()
    loads[6].wait()
    for layer in range(1, LAYERS):
        put_gram(2 * layer, xv[layer])
        put_gram(2 * layer + 1, gv[layer - 1])

    pl.semaphore_wait(barrier, greetings + jnp.where(on_diagonal, 0, 2))

    sent = []

    def send(src, dst, send_sem, recv_sem, target):
        copy = remote(src, dst, send_sem, recv_sem, target)
        copy.start()
        sent.append(copy)

    def wait_for(slot, send_sem, recv_sem):
        remote(slot, slot, send_sem, recv_sem, sibling).wait_recv()

    for off in range(1, NT):
        send(gp.at[t_at(off)], gr.at[tensor], gr_send.at[off], gr_recv.at[off], (dp, t_at(off)))

    def to_window(ref, send_sem, recv_sem):
        for wi, off in window_pairs:
            send(
                ref.at[0, y],
                ref.at[wi, y],
                send_sem.at[wi, off],
                recv_sem.at[wi, off],
                device(y_at(off), z_at(-WINDOW[wi]), x, c),
            )

    def from_window(ref, send_sem, recv_sem):
        for wi, off in window_pairs:
            wait_for(ref.at[wi, y_at(-off)], send_sem.at[wi, off], recv_sem.at[wi, off])

    to_window(hist, hist_send, hist_recv)

    def piece(wi, off):
        k = x_at(off)
        kind = lax.rem(z_at(-WINDOW[wi]), NW)
        first = k * PIECE
        row = 64 * (kind + NW * lax.div(first, 64)) + lax.rem(first, 64)
        return xt.at[pl.ds(pl.multiple_of(row, PIECE), PIECE)]

    def scatter(wi, off):
        k = x_at(off)
        return remote(
            piece(wi, off),
            xs.at[wi, y, k * 2 + c],
            sc_send.at[wi, off],
            sc_recv.at[wi, y],
            device(x, z_at(-WINDOW[wi]), k, c),
        )

    own_piece = pltpu.make_async_copy(piece(0, 0), xs.at[0, y, tensor], sc_recv.at[0, y])
    own_scatter = scatter(0, 0)

    @pl.when(jnp.logical_not(on_diagonal))
    def _():
        own_scatter.start()

    @pl.when(on_diagonal)
    def _():
        own_piece.start()

    for wi, off in piece_pairs:
        copy = scatter(wi, off)
        copy.start()
        sent.append(copy)

    for wi in range(1, NW):
        send(
            own_grads,
            gy.at[wi, y],
            gz_send.at[wi],
            gz_recv.at[wi],
            device(y, z_at(-WINDOW[wi]), x, c),
        )

    def grads_along_y(wi):
        block = gy.at[wi, y]
        send(block, block, gy_send.at[wi, 0], gy_recv.at[wi, 0], y_peer(1))
        send(block, block, gy_send.at[wi, 1], gy_recv.at[wi, 1], y_peer(-1))

    def grads_onward(wi):
        for way, step in ((0, 1), (1, -1)):
            block = gy.at[wi, y_at(-step)]
            wait_for(block, gy_send.at[wi, way], gy_recv.at[wi, way])
            half = gy.at[wi, y_at(-step), pl.ds(128 * way, 128)]
            send(half, half, gf_send.at[wi, way], gf_recv.at[wi, way], y_peer(step))

    grads_along_y(0)

    span = NW * NY // BLOCKS
    blocks = [(b * span // NY, b * span % NY) for b in range(BLOCKS)]

    def block_of(b, source_x, source_c):
        wi, first = blocks[b]
        return xs.at[wi, pl.ds(first, span), source_x * 2 + source_c]

    for b in range(BLOCKS):
        wi, first = blocks[b]
        for yy in range(first, first + span):
            wait_for(xs.at[wi, yy, tensor], sc_send.at[0, 0], sc_recv.at[wi, yy])
        block = block_of(b, x, c)
        send(block, block, ag_send.at[0, b], ag_recv.at[0, b], x_peer(1))
        send(block, block, ag_send.at[1, b], ag_recv.at[1, b], x_peer(-1))
        send(block, block, sib_send.at[0, b], sib_recv.at[0, b], sibling)

    from_window(hist, hist_send, hist_recv)
    window_count = hist[0, 0]
    for wi in range(NW):
        for yy in range(NY):
            if (wi, yy) != (0, 0):
                window_count = window_count + hist[wi, yy]
    ring[place] = window_count
    half_ring = members // 2

    def ring_send_step(s):
        down = ring.at[lax.rem(place + s, members)]
        send(down, down, ring_send.at[0, s], ring_recv.at[0, s], below)
        if s < members - 1 - half_ring:
            up = ring.at[lax.rem(place + members - s, members)]
            send(up, up, ring_send.at[1, s], ring_recv.at[1, s], above)

    def ring_wait_step(s):
        down = ring.at[lax.rem(place + s + 1, members)]
        wait_for(down, ring_send.at[0, s], ring_recv.at[0, s])
        if s < members - 1 - half_ring:
            up = ring.at[lax.rem(place + members - s - 1, members)]
            wait_for(up, ring_send.at[1, s], ring_recv.at[1, s])

    ring_send_step(0)
    grads_onward(0)

    total = gp[tensor].astype(F32)
    for off in range(1, NT):
        source = t_at(-off)
        wait_for(gr.at[source], gr_send.at[off], gr_recv.at[off])
        total = total + gr[source].astype(F32)
    product = total[0] * total[1] + total[2] * total[3] + total[4] * total[5]
    band = (16, 128)
    packed_row = lax.broadcasted_iota(jnp.int32, band, 0) + tensor * 16
    packed_lane = lax.broadcasted_iota(jnp.int32, band, 1)
    inner_row = lax.rem(packed_row, 64)
    inner_lane = lax.rem(packed_lane, 64)
    base = 64 * (2 * lax.div(packed_row, 64) + lax.div(packed_lane, 64))
    tok_t = base + inner_row
    tok_s = base + inner_lane + jnp.where(inner_lane >= inner_row, 0, 64)
    product = product * jnp.where(tok_t == tok_s, 1.0, 2.0)
    norm_part = jnp.zeros(tile, F32)
    for d in range(MAXDOC):
        inside = (
            (tok_t >= starts[d]) & (tok_t < ends[d]) & (tok_s >= starts[d]) & (tok_s < ends[d])
        )
        value = jnp.sum(jnp.where(inside, product, 0.0), keepdims=True)
        norm_part = jnp.where(sub8 == d, value, norm_part)
    npr[tensor] = norm_part
    for off in range(1, NT):
        send(
            npr.at[tensor], npr.at[tensor], np_send.at[off], np_recv.at[off], (dp, t_at(off))
        )

    for wi in range(1, NW):
        wait_for(gy.at[wi, y], gz_send.at[wi], gz_recv.at[wi])
        grads_along_y(wi)

    for b in range(BLOCKS):
        for hop, step in ((0, 1), (1, -1)):
            block = block_of(b, x_at(-step), c)
            wait_for(block, ag_send.at[hop, b], ag_recv.at[hop, b])
            if (b < BLOCKS // 2) == (hop == 0):
                send(block, block, ag_send.at[2, b], ag_recv.at[2, b], x_peer(step))
            send(block, block, sib_send.at[hop + 1, b], sib_recv.at[hop + 1, b], sibling)

    for s in range(half_ring):
        ring_wait_step(s)
        if s + 1 < half_ring:
            ring_send_step(s + 1)
    counts = ring[0]
    for m in range(1, members):
        counts = counts + ring[m]
    doc_count = jnp.sum(jnp.where(lane8 == patient_of, counts, 0.0), axis=1, keepdims=True)
    for off in range(1, NT):
        wait_for(npr.at[t_at(-off)], np_send.at[off], np_recv.at[off])
    norms = npr[0]
    for tt in range(1, NT):
        norms = norms + npr[tt]
    scale = clip_bound / jnp.maximum(clip_bound, jnp.sqrt(norms)) / jnp.maximum(doc_count, 1.0)
    position = lane8 + 128 * sub8
    weights = jnp.zeros(tile, F32)
    for d in range(MAXDOC):
        weights = jnp.where(
            (position >= starts[d]) & (position < ends[d]), scale[d : d + 1, :], weights
        )
    told[0, y] = weights
    to_window(told, told_send, told_recv)
    scale_row = jnp.sum(jnp.where(sub8 == lane8, scale, 0.0), axis=0, keepdims=True)
    scale_ref[...] = scale_row[:, :MAXDOC]

    for wi in range(1, NW):
        grads_onward(wi)

    for b in range(BLOCKS):
        block = block_of(b, x_at(2), c)
        wait_for(block, ag_send.at[2, b], ag_recv.at[2, b])
        send(block, block, sib_send.at[3, b], sib_recv.at[3, b], sibling)

    from_window(told, told_send, told_recv)
    columns = told[...].reshape(NW * NY * 8, 128).T
    for wi in range(NW):
        for way in range(2):
            half = gy.at[wi, y_at(2), pl.ds(128 * way, 128)]
            wait_for(half, gf_send.at[wi, way], gf_recv.at[wi, way])
        for yy in range(NY):
            for way in range(2):
                lane = (wi * NY + yy) * 8 + way
                rows = pl.ds(128 * way, 128)
                weight = columns[:, lane : lane + 1]
                wy[wi, yy, rows] = (weight * gy[wi, yy, rows].astype(F32)).astype(BF16)

    for hop, source_x in enumerate((x, x_at(-1), x_at(1), x_at(2))):
        for b in range(BLOCKS):
            wait_for(block_of(b, source_x, 1 - c), sib_send.at[hop, b], sib_recv.at[hop, b])

    sums = None
    for wi in range(NW):
        for yy in range(NY):
            features = xs[wi, yy].reshape(NT * PIECE, TOK)
            term = jnp.dot(features, wy[wi, yy], preferred_element_type=F32)
            sums = term if sums is None else sums + term
    step_rows = min(PIECE, 64)
    for tt in range(NT):
        for q in range(0, PIECE, step_rows):
            inner = (tt // 2) * PIECE + q
            owner = (tt % 2) * (8 // NW) + inner // 64
            first = tt * PIECE + q
            part[owner, inner % 64 : inner % 64 + step_rows] = sums[first : first + step_rows]

    rows = 64 // PIECES

    def down_steps(j):
        return half_ring - j % 2

    def chain_step(s, j, owner, arrivals, send_sem, recv_sem, target):
        at = pl.ds(j * rows, rows)
        mine = part.at[owner, at]
        if s > 0:
            slot = arrivals.at[s - 1, at]
            wait_for(slot, send_sem.at[s - 1, j], recv_sem.at[s - 1, j])
            mine[...] += slot[...]
        send(mine, arrivals.at[s, at], send_sem.at[s, j], recv_sem.at[s, j], target)

    for s in range(half_ring):
        for j in range(PIECES):
            down = down_steps(j)
            up = members - 1 - down
            if s < down:
                owner = lax.rem(place + members - down + s, members)
                chain_step(s, j, owner, rd, dn_send, dn_recv, below)
            if s < up:
                owner = lax.rem(place + up - s, members)
                chain_step(s, j, owner, ru, up_send, up_recv, above)
    for j in range(PIECES):
        at = pl.ds(j * rows, rows)
        down = down_steps(j)
        up = members - 1 - down
        value = part[place, at, :]
        if down > 0:
            slot = rd.at[down - 1, at]
            wait_for(slot, dn_send.at[down - 1, j], dn_recv.at[down - 1, j])
            value = value + slot[...]
        if up > 0:
            slot = ru.at[up - 1, at]
            wait_for(slot, up_send.at[up - 1, j], up_recv.at[up - 1, j])
            value = value + slot[...]
        out_ref[at, :] = value

    @pl.when(jnp.logical_not(on_diagonal))
    def _():
        own_scatter.wait_send()

    for copy in sent:
        copy.wait_send()


def on_device(nz, layer_inputs, layer_outgrads, doc_starts, row_tokens, doc_patient):
    clip_bound = DOC_MOST * math.sqrt(LAYERS * D * GW) / 300.0
    members = nz // NW
    half = members // 2
    vmem = pl.BlockSpec(memory_space=pltpu.VMEM)
    anywhere = pl.BlockSpec(memory_space=pl.ANY)
    dma = pltpu.SemaphoreType.DMA
    return pl.pallas_call(
        functools.partial(kernel, nz, clip_bound),
        out_shape=(
            jax.ShapeDtypeStruct((64, 256), F32),
            jax.ShapeDtypeStruct((1, MAXDOC), F32),
        ),
        in_specs=[anywhere] * 5,
        out_specs=(vmem, vmem),
        scratch_shapes=[
            pltpu.SMEM((1, MAXDOC), jnp.int32),
            pltpu.SMEM((1,), jnp.int32),
            pltpu.SMEM((1, MAXDOC), jnp.int32),
            pltpu.VMEM((LAYERS, TOK, 512), BF16),
            pltpu.VMEM((LAYERS - 1, TOK, 256), BF16),
            pltpu.VMEM((512, TOK), BF16),
            pltpu.VMEM((NW, NY, NT, PIECE, TOK), BF16),
            pltpu.VMEM((NW, NY, TOK, 256), BF16),
            pltpu.VMEM((NW, NY, TOK, 256), BF16),
            pltpu.VMEM((NT, 6, 16, 128), GRAM_TYPE),
            pltpu.VMEM((NT, 6, 16, 128), GRAM_TYPE),
            pltpu.VMEM((NT, 8, 128), F32),
            pltpu.VMEM((NW, NY, 8, 128), F32),
            pltpu.VMEM((members, 8, 128), F32),
            pltpu.VMEM((NW, NY, 8, 128), F32),
            pltpu.VMEM((members, 64, 256), F32),
            pltpu.VMEM((half, 64, 256), F32),
            pltpu.VMEM((half, 64, 256), F32),
            dma((7,)),
            dma((NW, NX)),
            dma((NW, NY)),
            dma((NW,)),
            dma((NW,)),
            dma((NW, 2)),
            dma((NW, 2)),
            dma((NW, 2)),
            dma((NW, 2)),
            dma((NW, NY)),
            dma((NW, NY)),
            dma((2, half)),
            dma((2, half)),
            dma((NT,)),
            dma((NT,)),
            dma((NT,)),
            dma((NT,)),
            dma((NW, NY)),
            dma((NW, NY)),
            dma((3, BLOCKS)),
            dma((3, BLOCKS)),
            dma((4, BLOCKS)),
            dma((4, BLOCKS)),
            dma((half, PIECES)),
            dma((half, PIECES)),
            dma((half, PIECES)),
            dma((half, PIECES)),
        ],
        compiler_params=pltpu.CompilerParams(
            collective_id=0, has_side_effects=True, vmem_limit_bytes=40 * 1024 * 1024
        ),
    )(layer_inputs, layer_outgrads, doc_starts, row_tokens, doc_patient)


def solution(mesh):
    placed = (
        P(None, "dp", "tensor"),
        P(None, "dp", "tensor"),
        P("dp", None),
        P("dp"),
        P("dp", None),
    )
    return jax.shard_map(
        functools.partial(on_device, mesh.shape["dp"] // NY),
        mesh=mesh,
        in_specs=placed,
        out_specs=(P("dp", "tensor"), P("dp", None)),
        check_vma=False,
    )
```

time: 880 us -> 64.9 us (0.07)
  the two profiles are of different devices: /device:TPU:2 before, /device:TPU:8 now
where the time goes in v2:
time: 64.9 us; the launch traced here: 64.7 us
  Pallas kernels  60 us (92%)
  local copies, waits for them, and re-layouts  3.27 us (5%)
  between operations  1.34 us (2%)
    pallas_call x1, Pallas kernels, on_device(): pl.pallas_call(functools.partial(kernel, nz, clip_bound), out_shape=(jax....  60 us
    unnamed x10, local copies, waits for them, and re-layouts  3.27 us

profile of v2, /device:TPU:8, one launch (start us, length us, event | category | flops | bytes accessed | tf_op | source)
XLA Modules:
  0.0 64.7 jit_solution(11193498677887901659)
XLA Ops:
  0.6 0.0 copy-start.3
  0.6 0.0 copy-start.2
  1.3 0.0 copy-done.3
  1.3 0.0 copy-done.2
  1.3 0.0 copy-start
  1.3 1.1 %copy-done = bf16[3,256,512]{2,1,0:T(8,128)(2,1)S(1)} copy-done((bf16[3,256,512]{2,1,0:T(8,128)(2,1)S(1)}, bf16[3,256,512]{2,1,0:T(8,128)(2,1)}, u32[]{:S(2)}) %copy-start) | copy-done | bytes 786456
  2.5 0.0 copy-start.1
  2.5 1.0 %copy-done.1 = bf16[3,256,256]{2,1,0:T(8,128)(2,1)S(1)} copy-done((bf16[3,256,256]{2,1,0:T(8,128)(2,1)S(1)}, bf16[3,256,256]{2,1,0:T(8,128)(2,1)}, u32[]{:S(2)}) %copy-start.1) | copy-done | bytes 393240
  3.5 60.0 %shard_map.68 = (f32[64,256]{1,0:T(8,128)S(1)}, f32[1,8]{1,0:T(1,128)S(1)}) custom-call(bf16[3,256,512]{2,1,0:T(8,128)(2,1)S(1)} %copy-done, bf16[3,256,256]{2,1,0:T(8,128)(2,1)S(1)} %copy-done.1, s32[1,8]{1,0:T(1,128)S(1)} %copy-done.2, s32[1]{0:T(128)S(6)} %copy.9.rows_in, s32[1,8]{1,0:T(1,128)S(1)} %copy-done.3), custom_call_target="tpu_custom_call" | custom-call | tf_op jit(solution)/shard_map/pallas_call | solution.py:517
  63.5 0.6 copy.10
  64.2 0.5 copy.11
Async XLA Ops:
  0.6 0.7 %copy-start.3 = (s32[1,8]{1,0:T(1,128)S(1)}, s32[1,8]{1,0:T(1,128)}, u32[]{:S(2)}) copy-start(s32[1,8]{1,0:T(1,128)} %pat_in.1) | copy-start | bytes 100
  0.6 0.7 %copy-start.2 = (s32[1,8]{1,0:T(1,128)S(1)}, s32[1,8]{1,0:T(1,128)}, u32[]{:S(2)}) copy-start(s32[1,8]{1,0:T(1,128)} %starts_in.1) | copy-start | bytes 100
  1.3 1.1 %copy-start = (bf16[3,256,512]{2,1,0:T(8,128)(2,1)S(1)}, bf16[3,256,512]{2,1,0:T(8,128)(2,1)}, u32[]{:S(2)}) copy-start(bf16[3,256,512]{2,1,0:T(8,128)(2,1)} %xi_ref.1) | copy-start | bytes 2359300
  2.5 1.0 %copy-start.1 = (bf16[3,256,256]{2,1,0:T(8,128)(2,1)S(1)}, bf16[3,256,256]{2,1,0:T(8,128)(2,1)}, u32[]{:S(2)}) copy-start(bf16[3,256,256]{2,1,0:T(8,128)(2,1)} %g_ref.1) | copy-start | bytes 1179652

commit v3 on v2

--- a/solution.py
+++ b/solution.py
@@ -17,12 +17,13 @@
 NX = 4
 NY = 4
 NT = 2 * NX
-WINDOW = (0, 1, -1, 2)
+WINDOW = (0, 1)
 NW = len(WINDOW)
 PIECE = 128 // NW
 BLOCKS = 4
 PIECES = 2
-GRAM_TYPE = jnp.float32
+VMEM_BYTES = 63283200
+GRAM_TYPE = jnp.bfloat16
 MESH = pl.DeviceIdType.MESH
 F32 = jnp.float32
 BF16 = jnp.bfloat16
@@ -90,8 +91,7 @@
     ring,
     told,
     part,
-    rd,
-    ru,
+    sums_in,
     in_sem,
     sc_send,
     sc_recv,
@@ -115,10 +115,8 @@
     ag_recv,
     sib_send,
     sib_recv,
-    dn_send,
-    dn_recv,
-    up_send,
-    up_recv,
+    sum_sent,
+    sum_recv,
 ):
     dp = lax.axis_index("dp")
     tensor = lax.axis_index("tensor")
@@ -126,7 +124,7 @@
     z = lax.rem(dp, nz)
     x = lax.div(tensor, 2)
     c = lax.rem(tensor, 2)
-    members = nz // NW
+    members = 8
     place = lax.div(z, NW)
 
     def device(yy, zz, xx, cc):
@@ -152,6 +150,7 @@
 
     sibling = device(y, z, x, 1 - c)
     below, above = device(y, z_at(-NW), x, c), device(y, z_at(NW), x, c)
+    below2, above2 = device(y, z_at(-2 * NW), x, c), device(y, z_at(2 * NW), x, c)
     on_diagonal = x == y
     window_pairs = [(wi, off) for wi in range(NW) for off in range(NY) if (wi, off) != (0, 0)]
     piece_pairs = [(wi, off) for wi in range(NW) for off in range(NX) if (wi, off) != (0, 0)]
@@ -163,21 +162,22 @@
 
     for off in range(1, NT):
         greet((dp, t_at(off)))
-    for wi, off in window_pairs:
-        greet(device(y_at(off), z_at(-WINDOW[wi]), x, c))
-        greet(device(y_at(-off), z_at(WINDOW[wi]), x, c))
+    window_peers = {(off, way * d) for d in WINDOW for way in (1, -1) for off in range(NY)}
+    window_peers = sorted(window_peers - {(0, 0)})
+    for off, d in window_peers:
+        greet(device(y_at(off), z_at(d), x, c))
     for wi, off in piece_pairs:
         greet(device(x, z_at(-WINDOW[wi]), x_at(off), c))
         greet(device(y_at(off), z_at(WINDOW[wi]), y, c))
-    greet(below)
-    greet(above)
+    for target in (below, above, below2, above2):
+        greet(target)
 
     @pl.when(jnp.logical_not(on_diagonal))
     def _():
         greet(device(x, z, x, c))
         greet(device(y, z, y, c))
 
-    greetings = NT - 1 + 2 * len(window_pairs) + 2 * len(piece_pairs) + 2
+    greetings = NT - 1 + len(window_peers) + 2 * len(piece_pairs) + 4
 
     own_grads = gy.at[0, y]
     loads = [
@@ -239,9 +239,6 @@
     def wait_for(slot, send_sem, recv_sem):
         remote(slot, slot, send_sem, recv_sem, sibling).wait_recv()
 
-    for off in range(1, NT):
-        send(gp.at[t_at(off)], gr.at[tensor], gr_send.at[off], gr_recv.at[off], (dp, t_at(off)))
-
     def to_window(ref, send_sem, recv_sem):
         for wi, off in window_pairs:
             send(
@@ -256,8 +253,6 @@
         for wi, off in window_pairs:
             wait_for(ref.at[wi, y_at(-off)], send_sem.at[wi, off], recv_sem.at[wi, off])
 
-    to_window(hist, hist_send, hist_recv)
-
     def piece(wi, off):
         k = x_at(off)
         kind = lax.rem(z_at(-WINDOW[wi]), NW)
@@ -275,6 +270,20 @@
             device(x, z_at(-WINDOW[wi]), k, c),
         )
 
+    def grads_along_y(wi):
+        block = gy.at[wi, y]
+        send(block, block, gy_send.at[wi, 0], gy_recv.at[wi, 0], y_peer(1))
+        send(block, block, gy_send.at[wi, 1], gy_recv.at[wi, 1], y_peer(-1))
+
+    def grads_onward(wi):
+        for way, step in ((0, 1), (1, -1)):
+            block = gy.at[wi, y_at(-step)]
+            wait_for(block, gy_send.at[wi, way], gy_recv.at[wi, way])
+            half = gy.at[wi, y_at(-step), pl.ds(128 * way, 128)]
+            send(half, half, gf_send.at[wi, way], gf_recv.at[wi, way], y_peer(step))
+
+    to_window(hist, hist_send, hist_recv)
+
     own_piece = pltpu.make_async_copy(piece(0, 0), xs.at[0, y, tensor], sc_recv.at[0, y])
     own_scatter = scatter(0, 0)
 
@@ -290,6 +299,10 @@
         copy = scatter(wi, off)
         copy.start()
         sent.append(copy)
+
+
+    for off in range(1, NT):
+        send(gp.at[t_at(off)], gr.at[tensor], gr_send.at[off], gr_recv.at[off], (dp, t_at(off)))
 
     for wi in range(1, NW):
         send(
@@ -300,17 +313,6 @@
             device(y, z_at(-WINDOW[wi]), x, c),
         )
 
-    def grads_along_y(wi):
-        block = gy.at[wi, y]
-        send(block, block, gy_send.at[wi, 0], gy_recv.at[wi, 0], y_peer(1))
-        send(block, block, gy_send.at[wi, 1], gy_recv.at[wi, 1], y_peer(-1))
-
-    def grads_onward(wi):
-        for way, step in ((0, 1), (1, -1)):
-            block = gy.at[wi, y_at(-step)]
-            wait_for(block, gy_send.at[wi, way], gy_recv.at[wi, way])
-            half = gy.at[wi, y_at(-step), pl.ds(128 * way, 128)]
-            send(half, half, gf_send.at[wi, way], gf_recv.at[wi, way], y_peer(step))
 
     grads_along_y(0)
 
@@ -330,30 +332,26 @@
         send(block, block, ag_send.at[1, b], ag_recv.at[1, b], x_peer(-1))
         send(block, block, sib_send.at[0, b], sib_recv.at[0, b], sibling)
 
+    for wi in range(1, NW):
+        wait_for(gy.at[wi, y], gz_send.at[wi], gz_recv.at[wi])
+        grads_along_y(wi)
+
     from_window(hist, hist_send, hist_recv)
     window_count = hist[0, 0]
     for wi in range(NW):
         for yy in range(NY):
             if (wi, yy) != (0, 0):
                 window_count = window_count + hist[wi, yy]
-    ring[place] = window_count
-    half_ring = members // 2
-
-    def ring_send_step(s):
-        down = ring.at[lax.rem(place + s, members)]
-        send(down, down, ring_send.at[0, s], ring_recv.at[0, s], below)
-        if s < members - 1 - half_ring:
-            up = ring.at[lax.rem(place + members - s, members)]
-            send(up, up, ring_send.at[1, s], ring_recv.at[1, s], above)
-
-    def ring_wait_step(s):
-        down = ring.at[lax.rem(place + s + 1, members)]
-        wait_for(down, ring_send.at[0, s], ring_recv.at[0, s])
-        if s < members - 1 - half_ring:
-            up = ring.at[lax.rem(place + members - s - 1, members)]
-            wait_for(up, ring_send.at[1, s], ring_recv.at[1, s])
-
-    ring_send_step(0)
+    ring[0] = window_count
+
+    def ring_send_to(slot, src, target):
+        send(ring.at[src], ring.at[slot], ring_send.at[slot], ring_recv.at[slot], target)
+
+    def ring_wait(slot):
+        wait_for(ring.at[slot], ring_send.at[slot], ring_recv.at[slot])
+
+    for slot, target in ((3, below2), (4, above2), (1, below), (2, above)):
+        ring_send_to(slot, 0, target)
     grads_onward(0)
 
     total = gp[tensor].astype(F32)
@@ -384,9 +382,11 @@
             npr.at[tensor], npr.at[tensor], np_send.at[off], np_recv.at[off], (dp, t_at(off))
         )
 
-    for wi in range(1, NW):
-        wait_for(gy.at[wi, y], gz_send.at[wi], gz_recv.at[wi])
-        grads_along_y(wi)
+    for slot in range(1, 5):
+        ring_wait(slot)
+    ring[5] = ring[1] + ring[3]
+    ring_send_to(6, 5, below2)
+    ring_send_to(7, 2, above2)
 
     for b in range(BLOCKS):
         for hop, step in ((0, 1), (1, -1)):
@@ -396,13 +396,14 @@
                 send(block, block, ag_send.at[2, b], ag_recv.at[2, b], x_peer(step))
             send(block, block, sib_send.at[hop + 1, b], sib_recv.at[hop + 1, b], sibling)
 
-    for s in range(half_ring):
-        ring_wait_step(s)
-        if s + 1 < half_ring:
-            ring_send_step(s + 1)
-    counts = ring[0]
-    for m in range(1, members):
-        counts = counts + ring[m]
+    for wi in range(1, NW):
+        grads_onward(wi)
+
+    ring_wait(6)
+    ring_wait(7)
+    counts = ring[0] + ring[6] + ring[7]
+    for slot in range(1, 5):
+        counts = counts + ring[slot]
     doc_count = jnp.sum(jnp.where(lane8 == patient_of, counts, 0.0), axis=1, keepdims=True)
     for off in range(1, NT):
         wait_for(npr.at[t_at(-off)], np_send.at[off], np_recv.at[off])
@@ -421,9 +422,6 @@
     scale_row = jnp.sum(jnp.where(sub8 == lane8, scale, 0.0), axis=0, keepdims=True)
     scale_ref[...] = scale_row[:, :MAXDOC]
 
-    for wi in range(1, NW):
-        grads_onward(wi)
-
     for b in range(BLOCKS):
         block = block_of(b, x_at(2), c)
         wait_for(block, ag_send.at[2, b], ag_recv.at[2, b])
@@ -462,42 +460,56 @@
 
     rows = 64 // PIECES
 
-    def down_steps(j):
-        return half_ring - j % 2
-
-    def chain_step(s, j, owner, arrivals, send_sem, recv_sem, target):
-        at = pl.ds(j * rows, rows)
-        mine = part.at[owner, at]
-        if s > 0:
-            slot = arrivals.at[s - 1, at]
-            wait_for(slot, send_sem.at[s - 1, j], recv_sem.at[s - 1, j])
-            mine[...] += slot[...]
-        send(mine, arrivals.at[s, at], send_sem.at[s, j], recv_sem.at[s, j], target)
-
-    for s in range(half_ring):
+    def owner_at(off):
+        return lax.rem(place + off + members, members)
+
+    def part_rows(off, j):
+        return part.at[owner_at(off), pl.ds(j * rows, rows)]
+
+    def arrival(slot, j):
+        return sums_in.at[slot, pl.ds(j * rows, rows)]
+
+    def sum_send(slot, j, off, target):
+        send(
+            part_rows(off, j),
+            arrival(slot, j),
+            sum_sent.at[slot, j],
+            sum_recv.at[slot, j],
+            target,
+        )
+
+    def sum_wait(slot, j):
+        wait_for(arrival(slot, j), sum_sent.at[slot, j], sum_recv.at[slot, j])
+        return arrival(slot, j)[...]
+
+    for j in range(PIECES):
+        if j % 2 == 0:
+            sum_send(2, j, 4, below2)
+        else:
+            sum_send(3, j, 4, above2)
+    for j in range(PIECES):
+        sum_send(0, j, -3, below)
+        sum_send(1, j, 3, above)
+    for j in range(PIECES):
+        sum_send(6, j, -1, below)
+        sum_send(7, j, 1, above)
+
+    for far in (False, True):
         for j in range(PIECES):
-            down = down_steps(j)
-            up = members - 1 - down
-            if s < down:
-                owner = lax.rem(place + members - down + s, members)
-                chain_step(s, j, owner, rd, dn_send, dn_recv, below)
-            if s < up:
-                owner = lax.rem(place + up - s, members)
-                chain_step(s, j, owner, ru, up_send, up_recv, above)
+            for way in range(2):
+                if far != (j % 2 == way):
+                    continue
+                near = (-2, 2)[way]
+                value = sum_wait(way, j)
+                if far:
+                    value = value + sum_wait(2 + way, j)
+                part_rows(near, j)[...] += value
+                sum_send(4 + way, j, near, (below2, above2)[way])
     for j in range(PIECES):
-        at = pl.ds(j * rows, rows)
-        down = down_steps(j)
-        up = members - 1 - down
-        value = part[place, at, :]
-        if down > 0:
-            slot = rd.at[down - 1, at]
-            wait_for(slot, dn_send.at[down - 1, j], dn_recv.at[down - 1, j])
-            value = value + slot[...]
-        if up > 0:
-            slot = ru.at[up - 1, at]
-            wait_for(slot, up_send.at[up - 1, j], up_recv.at[up - 1, j])
-            value = value + slot[...]
-        out_ref[at, :] = value
+        value = part[place, pl.ds(j * rows, rows), :]
+        for slot in (6, 7, 4, 5):
+            value = value + sum_wait(slot, j)
+        out_ref[pl.ds(j * rows, rows), :] = value
 
     @pl.when(jnp.logical_not(on_diagonal))
     def _():
@@ -510,7 +522,7 @@
 def on_device(nz, layer_inputs, layer_outgrads, doc_starts, row_tokens, doc_patient):
     clip_bound = DOC_MOST * math.sqrt(LAYERS * D * GW) / 300.0
     members = nz // NW
-    half = members // 2
+    assert members == 8
     vmem = pl.BlockSpec(memory_space=pltpu.VMEM)
     anywhere = pl.BlockSpec(memory_space=pl.ANY)
     dma = pltpu.SemaphoreType.DMA
@@ -536,11 +548,10 @@
             pltpu.VMEM((NT, 6, 16, 128), GRAM_TYPE),
             pltpu.VMEM((NT, 8, 128), F32),
             pltpu.VMEM((NW, NY, 8, 128), F32),
-            pltpu.VMEM((members, 8, 128), F32),
+            pltpu.VMEM((8, 8, 128), F32),
             pltpu.VMEM((NW, NY, 8, 128), F32),
             pltpu.VMEM((members, 64, 256), F32),
-            pltpu.VMEM((half, 64, 256), F32),
-            pltpu.VMEM((half, 64, 256), F32),
+            pltpu.VMEM((8, 64, 256), F32),
             dma((7,)),
             dma((NW, NX)),
             dma((NW, NY)),
@@ -552,8 +563,8 @@
             dma((NW, 2)),
             dma((NW, NY)),
             dma((NW, NY)),
-            dma((2, half)),
-            dma((2, half)),
+            dma((8,)),
+            dma((8,)),
             dma((NT,)),
             dma((NT,)),
             dma((NT,)),
@@ -564,13 +575,11 @@
             dma((3, BLOCKS)),
             dma((4, BLOCKS)),
             dma((4, BLOCKS)),
-            dma((half, PIECES)),
-            dma((half, PIECES)),
-            dma((half, PIECES)),
-            dma((half, PIECES)),
+            dma((8, PIECES)),
+            dma((8, PIECES)),
         ],
         compiler_params=pltpu.CompilerParams(
-            collective_id=0, has_side_effects=True, vmem_limit_bytes=40 * 1024 * 1024
+            collective_id=0, has_side_effects=True, vmem_limit_bytes=VMEM_BYTES
         ),
     )(layer_inputs, layer_outgrads, doc_starts, row_tokens, doc_patient)
 

time: 64.9 us -> 59 us (0.909)
  the two profiles are of different devices: /device:TPU:8 before, /device:TPU:4 now
where the time goes in v3:
time: 59 us; the launch traced here: 58.8 us
  Pallas kernels  55.5 us (94%)
  local copies, waits for them, and re-layouts  1.99 us (3%)
  between operations  1.29 us (2%)
    pallas_call x1, Pallas kernels, on_device(): pl.pallas_call(functools.partial(kernel, nz, clip_bound), out_shape=(jax....  55.5 us
    unnamed x4, local copies, waits for them, and re-layouts  1.99 us

profile of v3, /device:TPU:4, one launch (start us, length us, event | category | flops | bytes accessed | tf_op | source)
XLA Modules:
  0.0 58.8 jit_solution(4903994220124282058)
XLA Ops:
  1.3 55.5 %shard_map.68 = (f32[64,256]{1,0:T(8,128)}, f32[1,8]{1,0:T(1,128)}) custom-call(bf16[3,256,512]{2,1,0:T(8,128)(2,1)} %xi_ref.1, bf16[3,256,256]{2,1,0:T(8,128)(2,1)} %g_ref.1, s32[1,8]{1,0:T(1,128)} %starts_in.1, s32[1]{0:T(128)S(6)} %copy.9.rows_in, s32[1,8]{1,0:T(1,128)} %pat_in.1), custom_call_target="tpu_custom_call" | custom-call | tf_op jit(solution)/shard_map/pallas_call | solution.py:529
  56.8 0.0 copy-start
  56.8 1.5 %copy.10 = f32[64,256]{1,0:T(8,128)} copy(f32[64,256]{1,0:T(8,128)} %get-tuple-element.4) | data formatting | bytes 131072
  58.3 0.0 copy-done
  58.3 0.5 copy.11
Async XLA Ops:
  56.8 1.5 %copy-start = (f32[1,8]{1,0:T(1,128)S(1)}, f32[1,8]{1,0:T(1,128)}, u32[]{:S(2)}) copy-start(f32[1,8]{1,0:T(1,128)} %get-tuple-element.5) | copy-start | bytes 100

commit v4 on v3

--- a/solution.py
+++ b/solution.py
@@ -316,6 +316,23 @@
 
     grads_along_y(0)
 
+    from_window(hist, hist_send, hist_recv)
+    window_count = hist[0, 0]
+    for wi in range(NW):
+        for yy in range(NY):
+            if (wi, yy) != (0, 0):
+                window_count = window_count + hist[wi, yy]
+    ring[0] = window_count
+
+    def ring_send_to(slot, src, target):
+        send(ring.at[src], ring.at[slot], ring_send.at[slot], ring_recv.at[slot], target)
+
+    def ring_wait(slot):
+        wait_for(ring.at[slot], ring_send.at[slot], ring_recv.at[slot])
+
+    for slot, target in ((3, below2), (4, above2), (1, below), (2, above)):
+        ring_send_to(slot, 0, target)
+
     span = NW * NY // BLOCKS
     blocks = [(b * span // NY, b * span % NY) for b in range(BLOCKS)]
 
@@ -336,22 +353,6 @@
         wait_for(gy.at[wi, y], gz_send.at[wi], gz_recv.at[wi])
         grads_along_y(wi)
 
-    from_window(hist, hist_send, hist_recv)
-    window_count = hist[0, 0]
-    for wi in range(NW):
-        for yy in range(NY):
-            if (wi, yy) != (0, 0):
-                window_count = window_count + hist[wi, yy]
-    ring[0] = window_count
-
-    def ring_send_to(slot, src, target):
-        send(ring.at[src], ring.at[slot], ring_send.at[slot], ring_recv.at[slot], target)
-
-    def ring_wait(slot):
-        wait_for(ring.at[slot], ring_send.at[slot], ring_recv.at[slot])
-
-    for slot, target in ((3, below2), (4, above2), (1, below), (2, above)):
-        ring_send_to(slot, 0, target)
     grads_onward(0)
 
     total = gp[tensor].astype(F32)

time: 59 us -> 57.2 us (0.969)
  the two profiles are of different devices: /device:TPU:4 before, /device:TPU:32 now
where the time goes in v4:
time: 57.2 us; the launch traced here: 57 us
  Pallas kernels  53.8 us (94%)
  local copies, waits for them, and re-layouts  1.99 us (3%)
  between operations  1.29 us (2%)
    pallas_call x1, Pallas kernels, on_device(): pl.pallas_call(functools.partial(kernel, nz, clip_bound), out_shape=(jax....  53.8 us
    unnamed x4, local copies, waits for them, and re-layouts  1.99 us

profile of v4, /device:TPU:32, one launch (start us, length us, event | category | flops | bytes accessed | tf_op | source)
XLA Modules:
  0.0 57.0 jit_solution(13727424868719388239)
XLA Ops:
  1.3 53.8 %shard_map.68 = (f32[64,256]{1,0:T(8,128)}, f32[1,8]{1,0:T(1,128)}) custom-call(bf16[3,256,512]{2,1,0:T(8,128)(2,1)} %xi_ref.1, bf16[3,256,256]{2,1,0:T(8,128)(2,1)} %g_ref.1, s32[1,8]{1,0:T(1,128)} %starts_in.1, s32[1]{0:T(128)S(6)} %copy.9.rows_in, s32[1,8]{1,0:T(1,128)} %pat_in.1), custom_call_target="tpu_custom_call" | custom-call | tf_op jit(solution)/shard_map/pallas_call | solution.py:530
  55.0 0.0 copy-start
  55.1 1.5 %copy.10 = f32[64,256]{1,0:T(8,128)} copy(f32[64,256]{1,0:T(8,128)} %get-tuple-element.4) | data formatting | bytes 131072
  56.5 0.0 copy-done
  56.5 0.5 copy.11
Async XLA Ops:
  55.0 1.5 %copy-start = (f32[1,8]{1,0:T(1,128)S(1)}, f32[1,8]{1,0:T(1,128)}, u32[]{:S(2)}) copy-start(f32[1,8]{1,0:T(1,128)} %get-tuple-element.5) | copy-start | bytes 100

commit v5 on v4

--- a/solution.py
+++ b/solution.py
@@ -83,7 +83,6 @@
     xt,
     xs,
     gy,
-    wy,
     gp,
     gr,
     npr,
@@ -434,12 +433,6 @@
         for way in range(2):
             half = gy.at[wi, y_at(2), pl.ds(128 * way, 128)]
             wait_for(half, gf_send.at[wi, way], gf_recv.at[wi, way])
-        for yy in range(NY):
-            for way in range(2):
-                lane = (wi * NY + yy) * 8 + way
-                rows = pl.ds(128 * way, 128)
-                weight = columns[:, lane : lane + 1]
-                wy[wi, yy, rows] = (weight * gy[wi, yy, rows].astype(F32)).astype(BF16)
 
     for hop, source_x in enumerate((x, x_at(-1), x_at(1), x_at(2))):
         for b in range(BLOCKS):
@@ -449,7 +442,10 @@
     for wi in range(NW):
         for yy in range(NY):
             features = xs[wi, yy].reshape(NT * PIECE, TOK)
-            term = jnp.dot(features, wy[wi, yy], preferred_element_type=F32)
+            lane = (wi * NY + yy) * 8
+            weight = jnp.concatenate([columns[:, lane : lane + 1], columns[:, lane + 1 : lane + 2]])
+            weighted = (weight * gy[wi, yy].astype(F32)).astype(BF16)
+            term = jnp.dot(features, weighted, preferred_element_type=F32)
             sums = term if sums is None else sums + term
     step_rows = min(PIECE, 64)
     for tt in range(NT):
@@ -543,7 +539,6 @@
             pltpu.VMEM((LAYERS - 1, TOK, 256), BF16),
             pltpu.VMEM((512, TOK), BF16),
             pltpu.VMEM((NW, NY, NT, PIECE, TOK), BF16),
-            pltpu.VMEM((NW, NY, TOK, 256), BF16),
             pltpu.VMEM((NW, NY, TOK, 256), BF16),
             pltpu.VMEM((NT, 6, 16, 128), GRAM_TYPE),
             pltpu.VMEM((NT, 6, 16, 128), GRAM_TYPE),

time: 57.2 us -> 56.9 us (level)
  no operation moved by 1% of the time
where the time goes in v5:
time: 56.9 us; the launch traced here: 56.7 us
  Pallas kernels  53.4 us (94%)
  local copies, waits for them, and re-layouts  1.99 us (3%)
  between operations  1.29 us (2%)
    pallas_call x1, Pallas kernels, on_device(): pl.pallas_call(functools.partial(kernel, nz, clip_bound), out_shape=(jax....  53.4 us
    unnamed x4, local copies, waits for them, and re-layouts  1.99 us

profile of v5, /device:TPU:32, one launch (start us, length us, event | category | flops | bytes accessed | tf_op | source)
XLA Modules:
  0.0 56.7 jit_solution(6943227597847988069)
XLA Ops:
  1.3 53.4 %shard_map.68 = (f32[64,256]{1,0:T(8,128)}, f32[1,8]{1,0:T(1,128)}) custom-call(bf16[3,256,512]{2,1,0:T(8,128)(2,1)} %xi_ref.1, bf16[3,256,256]{2,1,0:T(8,128)(2,1)} %g_ref.1, s32[1,8]{1,0:T(1,128)} %starts_in.1, s32[1]{0:T(128)S(6)} %copy.9.rows_in, s32[1,8]{1,0:T(1,128)} %pat_in.1), custom_call_target="tpu_custom_call" | custom-call | tf_op jit(solution)/shard_map/pallas_call | solution.py:526
  54.7 0.0 copy-start
  54.7 1.5 %copy.10 = f32[64,256]{1,0:T(8,128)} copy(f32[64,256]{1,0:T(8,128)} %get-tuple-element.4) | data formatting | bytes 131072
  56.2 0.0 copy-done
  56.2 0.5 copy.11
Async XLA Ops:
  54.7 1.5 %copy-start = (f32[1,8]{1,0:T(1,128)S(1)}, f32[1,8]{1,0:T(1,128)}, u32[]{:S(2)}) copy-start(f32[1,8]{1,0:T(1,128)} %get-tuple-element.5) | copy-start | bytes 100

commit v6 on v4

--- a/solution.py
+++ b/solution.py
@@ -21,7 +21,7 @@
 NW = len(WINDOW)
 PIECE = 128 // NW
 BLOCKS = 4
-PIECES = 2
+PIECES = 4
 VMEM_BYTES = 63283200
 GRAM_TYPE = jnp.bfloat16
 MESH = pl.DeviceIdType.MESH
@@ -340,7 +340,7 @@
         wi, first = blocks[b]
         return xs.at[wi, pl.ds(first, span), source_x * 2 + source_c]
 
-    for b in range(BLOCKS):
+    for b in range(BLOCKS // 2):
         wi, first = blocks[b]
         for yy in range(first, first + span):
             wait_for(xs.at[wi, yy, tensor], sc_send.at[0, 0], sc_recv.at[wi, yy])
@@ -349,11 +349,20 @@
         send(block, block, ag_send.at[1, b], ag_recv.at[1, b], x_peer(-1))
         send(block, block, sib_send.at[0, b], sib_recv.at[0, b], sibling)
 
+    grads_onward(0)
+    for b in range(BLOCKS // 2, BLOCKS):
+        wi, first = blocks[b]
+        for yy in range(first, first + span):
+            wait_for(xs.at[wi, yy, tensor], sc_send.at[0, 0], sc_recv.at[wi, yy])
+        block = block_of(b, x, c)
+        send(block, block, ag_send.at[0, b], ag_recv.at[0, b], x_peer(1))
+        send(block, block, ag_send.at[1, b], ag_recv.at[1, b], x_peer(-1))
+        send(block, block, sib_send.at[0, b], sib_recv.at[0, b], sibling)
+
     for wi in range(1, NW):
         wait_for(gy.at[wi, y], gz_send.at[wi], gz_recv.at[wi])
         grads_along_y(wi)
 
-    grads_onward(0)
 
     total = gp[tensor].astype(F32)
     for off in range(1, NT):

time: 57.2 us -> 58.5 us (1.023)
  the two profiles are of different devices: /device:TPU:32 before, /device:TPU:2 now
where the time goes in v6:
time: 58.5 us; the launch traced here: 58.3 us
  Pallas kernels  55 us (94%)
  local copies, waits for them, and re-layouts  1.99 us (3%)
  between operations  1.29 us (2%)
    pallas_call x1, Pallas kernels, on_device(): pl.pallas_call(functools.partial(kernel, nz, clip_bound), out_shape=(jax....  55 us
    unnamed x4, local copies, waits for them, and re-layouts  1.99 us

profile of v6, /device:TPU:2, one launch (start us, length us, event | category | flops | bytes accessed | tf_op | source)
XLA Modules:
  0.0 58.3 jit_solution(5365087065626255512)
XLA Ops:
  1.3 55.0 %shard_map.68 = (f32[64,256]{1,0:T(8,128)}, f32[1,8]{1,0:T(1,128)}) custom-call(bf16[3,256,512]{2,1,0:T(8,128)(2,1)} %xi_ref.1, bf16[3,256,256]{2,1,0:T(8,128)(2,1)} %g_ref.1, s32[1,8]{1,0:T(1,128)} %starts_in.1, s32[1]{0:T(128)S(6)} %copy.9.rows_in, s32[1,8]{1,0:T(1,128)} %pat_in.1), custom_call_target="tpu_custom_call" | custom-call | tf_op jit(solution)/shard_map/pallas_call | solution.py:539
  56.3 0.0 copy-start
  56.3 1.5 %copy.10 = f32[64,256]{1,0:T(8,128)} copy(f32[64,256]{1,0:T(8,128)} %get-tuple-element.4) | data formatting | bytes 131072
  57.8 0.0 copy-done
  57.8 0.5 copy.11
Async XLA Ops:
  56.3 1.5 %copy-start = (f32[1,8]{1,0:T(1,128)S(1)}, f32[1,8]{1,0:T(1,128)}, u32[]{:S(2)}) copy-start(f32[1,8]{1,0:T(1,128)} %get-tuple-element.5) | copy-start | bytes 100
